TPU v7x, 512 devices: a whole 4x4x16 slice. The times are simulated.
512 devices in a mesh: grp: 64 (over z_lo, y, core), tile: 8 (over z_hi, x).
Axes of the slice: x: 4, y: 4, z: 16 (z_hi: 2, z_lo: 8; z = z_hi * 8 + z_lo), core: 2. Of those that a mesh axis runs over, the one named last changes fastest.
Arguments:
- points: float32 [3, 65536], P(None, ('grp', 'tile')), may hold values from 0 to 4
- probes: bfloat16 [8, 65536], P(None, ('grp', 'tile')), may hold values from -1 to 1
Outputs:
- products: float32 [3, 8, 65536], P(None, None, ('grp', 'tile'))
All inputs are finite; a program needn't handle non-finite values.
Results may differ from a plain program's by a relative error of at most 0.0029.
Values may be sent and summed in bfloat16 or wider, within the bound.
No kernel may reach another device: no remote copies, remote signals or barrier semaphores. Data moves between devices by JAX's collectives and lax.ppermute only.
A program may use at most 64 MiB of HBM per device.

v0:
```python
import jax
import jax.numpy as jnp
from jax import lax
from jax.sharding import PartitionSpec as P

ROUNDS = 4


def from_behind(block, axis, distance):
    devices = range(lax.axis_size(axis))
    route = [((i - distance) % len(devices), i) for i in devices]
    return lax.ppermute(block, axis, route)


def tile_kernels(row_points, col_points):
    diffs = row_points[:, :, None] - col_points[:, None, :]
    flat_q = (diffs[0] * diffs[0] + diffs[1] * diffs[1]) / (0.35 * 0.35)
    depth_q = diffs[2] * diffs[2] / (0.25 * 0.25)
    scaled = jnp.sqrt(3.0 * (flat_q + depth_q) + 1e-06)
    decay = 1.3 * jnp.exp(-scaled)
    stacked = jnp.stack([(1.0 + scaled) * decay, 3.0 * flat_q * decay, 3.0 * depth_q * decay])
    return stacked.astype(jnp.bfloat16)


def forward_terms(kernels, col_probe):
    return jnp.einsum("kmn,pn->kpm", kernels, col_probe, preferred_element_type=jnp.float32)


def body(points, probes):
    result_sum = jnp.zeros((3, probes.shape[0], points.shape[1]), jnp.float32)
    group_pts = lax.all_gather(points, "tile", axis=1, tiled=True)
    group_probe = lax.all_gather(probes, "tile", axis=1, tiled=True)
    for offset in range(1, ROUNDS + 1):
        far_pts = from_behind(group_pts, "grp", -offset)
        far_probe = from_behind(group_probe, "grp", -offset)
        kernels = tile_kernels(points, far_pts)
        result_sum = result_sum + forward_terms(kernels, far_probe)
        mirror_terms = jnp.einsum(
            "kmn,pm->kpn", kernels, probes, preferred_element_type=jnp.float32
        )
        share_terms = lax.psum_scatter(mirror_terms, "tile", scatter_dimension=2, tiled=True)
        result_sum = result_sum + from_behind(share_terms, "grp", offset)
    return result_sum


def solution(mesh):
    return jax.shard_map(
        body,
        mesh=mesh,
        in_specs=(P(None, ("grp", "tile")), P(None, ("grp", "tile"))),
        out_specs=P(None, None, ("grp", "tile")),
        check_vma=False,
    )
```

profile of v0, /device:TPU:1, one launch (start us, length us, event | category | flops | bytes accessed | tf_op | source)
XLA Modules:
  0.0 583.4 jit_solution(7496651568663367594)
XLA Ops:
  6.5 58.8 %all_gather.6 = f32[3,1024]{1,0:T(4,128)S(1)} all-gather(f32[3,128]{1,0:T(4,128)} %param.2), channel_id=1, replica_groups=mesh['grp'=64,'tile'=8] {'tile'}, dimensions={1}, use_global_device_ids=true | all-gather | bytes 13824 | tf_op jit(solution)/shard_map/all_gather | solution.py:31
  65.4 8.6 %collective-permute-start = (f32[3,1024]{1,0:T(4,128)S(1)}, f32[3,1024]{1,0:T(4,128)S(1)}, u32[]{:S(2)}, u32[]{:S(2)}) collective-permute-start(f32[3,1024]{1,0:T(4,128)S(1)} %all_gather.6), channel_id=1, source_target_pairs={{8,0},{16,8},{24,16},{32,24},{40,32},{48,40},{56,48},{64,56},{72,6... | collective-permute-start | bytes 36872 | tf_op jit(solution)/shard_map/ppermute | solution.py:12
  73.9 10.0 %collective-permute-start.3 = (f32[3,1024]{1,0:T(4,128)S(1)}, f32[3,1024]{1,0:T(4,128)S(1)}, u32[]{:S(2)}, u32[]{:S(2)}) collective-permute-start(f32[3,1024]{1,0:T(4,128)S(1)} %all_gather.6), channel_id=1, source_target_pairs={{16,0},{24,8},{32,16},{40,24},{48,32},{56,40},{64,48},{72,56},{80,... | collective-permute-start | bytes 36872 | tf_op jit(solution)/shard_map/ppermute | solution.py:12
  83.9 2.5 collective-permute-start.6
  86.5 2.0 collective-permute-start.9
  88.4 54.0 %all_gather.7 = bf16[8,1024]{1,0:T(8,128)(2,1)S(1)} all-gather(bf16[8,128]{1,0:T(8,128)(2,1)} %param.3), channel_id=1, replica_groups=mesh['grp'=64,'tile'=8] {'tile'}, dimensions={1}, use_global_device_ids=true | all-gather | bytes 18432 | tf_op jit(solution)/shard_map/all_gather | solution.py:32
  142.5 4.8 collective-permute-start.4
  147.3 0.0 collective-permute-done
  147.3 6.9 %collective-permute-start.7 = (bf16[8,1024]{1,0:T(8,128)(2,1)S(1)}, bf16[8,1024]{1,0:T(8,128)(2,1)S(1)}, u32[]{:S(2)}, u32[]{:S(2)}) collective-permute-start(bf16[8,1024]{1,0:T(8,128)(2,1)S(1)} %all_gather.7), channel_id=1, source_target_pairs={{24,0},{32,8},{40,16},{48,24},{56,32},{64,40},{72,48},{80,56},{88,... | collective-permute-start | bytes 49160 | tf_op jit(solution)/shard_map/ppermute | solution.py:12
  154.2 0.0 collective-permute-done.3
  154.2 4.1 collective-permute-start.10
  158.3 0.0 collective-permute-done.6
  158.3 1.9 collective-permute-start.1
  160.2 0.0 collective-permute-done.9
  160.2 2.6 broadcast_subtract_fusion.3
  162.8 0.4 multiply_convert_fusion.11
  163.2 0.0 copy-start.14
  163.2 0.2 multiply_convert_fusion.10
  163.4 0.0 copy-start.1
  163.5 0.0 copy-start.3
  163.5 0.7 copy-done.1
  164.1 0.1 copy-done.3
  164.2 0.9 convolution_bitcast_fusion.3
  165.1 0.0 reduce-scatter.5.cloned.1.call-update
  165.1 0.0 reduce-scatter.7.cloned.1.call-start
  165.2 1.9 multiply_convert_fusion.8
  167.0 0.0 copy-done
  167.1 0.2 multiply_convert_fusion.7
  167.3 1.1 multiply_convert_fusion.5
  168.4 1.1 multiply_convert_fusion.4
  169.4 0.4 multiply_convert_fusion.2
  169.8 0.2 multiply_convert_fusion.1
  170.1 0.9 convolution_bitcast_fusion.2
  171.0 0.0 reduce-scatter.7.cloned.1.call-update
  171.0 0.0 reduce-scatter.9.cloned.1.call-start
  171.1 0.0 copy-done.12
  171.1 0.1 copy-done.13
  171.2 0.9 convolution_bitcast_fusion.1
  172.1 0.0 reduce-scatter.9.cloned.1.call-update
  172.1 0.0 reduce-scatter.11.cloned.1.call-start
  172.1 0.9 convolution_bitcast_fusion
  173.0 0.0 reduce-scatter.11.cloned.1.call-update
  173.0 0.0 collective-permute-done.4
  173.0 0.0 copy-done.9
  173.1 0.1 copy-done.11
  173.2 0.3 convolution_bitcast_fusion.6
  173.5 0.0 collective-permute-done.7
  173.5 0.3 convolution_bitcast_fusion.5
  173.8 88.3 %reduce-scatter.5.cloned.1.call-done = f32[3,8,128]{2,1,0:T(8,128)} async-done(((f32[3,8,1024]{2,1,0:T(8,128)}), f32[3,8,128]{2,1,0:T(8,128)}) %reduce-scatter.5.cloned.1.call-update) | async-done | bytes 12304 | tf_op jit(solution)/shard_map/reduce_scatter | solution.py:41
  262.1 5.6 collective-permute-start.2
  267.7 94.5 %reduce-scatter.7.cloned.1.call-done = f32[3,8,128]{2,1,0:T(8,128)} async-done(((f32[3,8,1024]{2,1,0:T(8,128)}), f32[3,8,128]{2,1,0:T(8,128)}) %reduce-scatter.7.cloned.1.call-update) | async-done | bytes 12304 | tf_op jit(solution)/shard_map/reduce_scatter | solution.py:41
  362.3 3.0 collective-permute-start.5
  365.3 97.0 %reduce-scatter.9.cloned.1.call-done = f32[3,8,128]{2,1,0:T(8,128)} async-done(((f32[3,8,1024]{2,1,0:T(8,128)}), f32[3,8,128]{2,1,0:T(8,128)}) %reduce-scatter.9.cloned.1.call-update) | async-done | bytes 12304 | tf_op jit(solution)/shard_map/reduce_scatter | solution.py:41
  462.3 7.0 %collective-permute-start.8 = (f32[3,8,128]{2,1,0:T(8,128)}, f32[3,8,128]{2,1,0:T(8,128)S(1)}, u32[]{:S(2)}, u32[]{:S(2)}) collective-permute-start(f32[3,8,128]{2,1,0:T(8,128)} %reduce-scatter.9.cloned.1.call-done), channel_id=1, source_target_pairs={{488,0},{496,8},{504,16},{0,24},{8,32},{16,40},{24,48},{32,56},{40... | collective-permute-start | bytes 36872 | tf_op jit(solution)/shard_map/ppermute | solution.py:12
  469.4 0.0 collective-permute-done.10
  469.4 92.9 %reduce-scatter.11.cloned.1.call-done = f32[3,8,128]{2,1,0:T(8,128)} async-done(((f32[3,8,1024]{2,1,0:T(8,128)}), f32[3,8,128]{2,1,0:T(8,128)}) %reduce-scatter.11.cloned.1.call-update) | async-done | bytes 12304 | tf_op jit(solution)/shard_map/reduce_scatter | solution.py:41
  562.3 4.6 collective-permute-start.11
  566.9 0.3 convolution_bitcast_fusion.4
  567.2 0.0 collective-permute-done.1
  567.2 0.0 collective-permute-done.2
  567.2 0.0 collective-permute-done.5
  567.3 0.0 collective-permute-done.8
  567.3 8.6 %collective-permute-done.11 = f32[3,8,128]{2,1,0:T(8,128)S(1)} collective-permute-done((f32[3,8,128]{2,1,0:T(8,128)}, f32[3,8,128]{2,1,0:T(8,128)S(1)}, u32[]{:S(2)}, u32[]{:S(2)}) %collective-permute-start.11) | collective-permute-done | bytes 12320 | tf_op jit(solution)/shard_map/ppermute | solution.py:12
  575.9 0.9 fusion.6
  (21 shorter events, 0.0 us)
Async XLA Ops:
  6.5 255.6 %reduce-scatter.5.cloned.1.call-start = ((), (), s32[]{:S(2)}) async-start(), calls=%async_computation.4 | async-start | bytes 110592 | tf_op jit(solution)/shard_map/reduce_scatter | solution.py:41
  65.4 81.9 %collective-permute-start = (f32[3,1024]{1,0:T(4,128)S(1)}, f32[3,1024]{1,0:T(4,128)S(1)}, u32[]{:S(2)}, u32[]{:S(2)}) collective-permute-start(f32[3,1024]{1,0:T(4,128)S(1)} %all_gather.6), channel_id=1, source_target_pairs={{8,0},{16,8},{24,16},{32,24},{40,32},{48,40},{56,48},{64,56},{72,6... | collective-permute-start | bytes 36872 | tf_op jit(solution)/shard_map/ppermute | solution.py:12
  73.9 80.3 %collective-permute-start.3 = (f32[3,1024]{1,0:T(4,128)S(1)}, f32[3,1024]{1,0:T(4,128)S(1)}, u32[]{:S(2)}, u32[]{:S(2)}) collective-permute-start(f32[3,1024]{1,0:T(4,128)S(1)} %all_gather.6), channel_id=1, source_target_pairs={{16,0},{24,8},{32,16},{40,24},{48,32},{56,40},{64,48},{72,56},{80,... | collective-permute-start | bytes 36872 | tf_op jit(solution)/shard_map/ppermute | solution.py:12
  83.9 74.4 %collective-permute-start.6 = (f32[3,1024]{1,0:T(4,128)S(1)}, f32[3,1024]{1,0:T(4,128)S(1)}, u32[]{:S(2)}, u32[]{:S(2)}) collective-permute-start(f32[3,1024]{1,0:T(4,128)S(1)} %all_gather.6), channel_id=1, source_target_pairs={{24,0},{32,8},{40,16},{48,24},{56,32},{64,40},{72,48},{80,56},{88,... | collective-permute-start | bytes 36872 | tf_op jit(solution)/shard_map/ppermute | solution.py:12
  86.5 73.8 %collective-permute-start.9 = (f32[3,1024]{1,0:T(4,128)S(1)}, f32[3,1024]{1,0:T(4,128)S(1)}, u32[]{:S(2)}, u32[]{:S(2)}) collective-permute-start(f32[3,1024]{1,0:T(4,128)S(1)} %all_gather.6), channel_id=1, source_target_pairs={{32,0},{40,8},{48,16},{56,24},{64,32},{72,40},{80,48},{88,56},{96,... | collective-permute-start | bytes 36872 | tf_op jit(solution)/shard_map/ppermute | solution.py:12
  142.5 30.5 %collective-permute-start.4 = (bf16[8,1024]{1,0:T(8,128)(2,1)S(1)}, bf16[8,1024]{1,0:T(8,128)(2,1)S(1)}, u32[]{:S(2)}, u32[]{:S(2)}) collective-permute-start(bf16[8,1024]{1,0:T(8,128)(2,1)S(1)} %all_gather.7), channel_id=1, source_target_pairs={{16,0},{24,8},{32,16},{40,24},{48,32},{56,40},{64,48},{72,56},{80,... | collective-permute-start | bytes 49160 | tf_op jit(solution)/shard_map/ppermute | solution.py:12
  147.3 26.2 %collective-permute-start.7 = (bf16[8,1024]{1,0:T(8,128)(2,1)S(1)}, bf16[8,1024]{1,0:T(8,128)(2,1)S(1)}, u32[]{:S(2)}, u32[]{:S(2)}) collective-permute-start(bf16[8,1024]{1,0:T(8,128)(2,1)S(1)} %all_gather.7), channel_id=1, source_target_pairs={{24,0},{32,8},{40,16},{48,24},{56,32},{64,40},{72,48},{80,56},{88,... | collective-permute-start | bytes 49160 | tf_op jit(solution)/shard_map/ppermute | solution.py:12
  154.2 315.2 %collective-permute-start.10 = (bf16[8,1024]{1,0:T(8,128)(2,1)S(1)}, bf16[8,1024]{1,0:T(8,128)(2,1)S(1)}, u32[]{:S(2)}, u32[]{:S(2)}) collective-permute-start(bf16[8,1024]{1,0:T(8,128)(2,1)S(1)} %all_gather.7), channel_id=1, source_target_pairs={{32,0},{40,8},{48,16},{56,24},{64,32},{72,40},{80,48},{88,56},{96,... | collective-permute-start | bytes 49160 | tf_op jit(solution)/shard_map/ppermute | solution.py:12
  158.3 408.9 %collective-permute-start.1 = (bf16[8,1024]{1,0:T(8,128)(2,1)S(1)}, bf16[8,1024]{1,0:T(8,128)(2,1)S(1)}, u32[]{:S(2)}, u32[]{:S(2)}) collective-permute-start(bf16[8,1024]{1,0:T(8,128)(2,1)S(1)} %all_gather.7), channel_id=1, source_target_pairs={{8,0},{16,8},{24,16},{32,24},{40,32},{48,40},{56,48},{64,56},{72,6... | collective-permute-start | bytes 49160 | tf_op jit(solution)/shard_map/ppermute | solution.py:12
  163.2 1.1 copy-start.14
  163.4 0.7 copy-start.1
  163.5 0.8 copy-start.3
  165.1 197.2 %reduce-scatter.7.cloned.1.call-start = ((), (), s32[]{:S(2)}) async-start(), calls=%async_computation.5 | async-start | bytes 110592 | tf_op jit(solution)/shard_map/reduce_scatter | solution.py:41
  165.2 1.9 copy-start
  167.0 3.1 copy-start.5
  167.3 2.8 copy-start.8
  167.3 2.8 copy-start.10
  170.1 1.0 copy-start.7
  170.1 1.0 copy-start.12
  170.1 1.1 copy-start.13
  171.0 291.3 %reduce-scatter.9.cloned.1.call-start = ((), (), s32[]{:S(2)}) async-start(), calls=%async_computation.6 | async-start | bytes 110592 | tf_op jit(solution)/shard_map/reduce_scatter | solution.py:41
  172.0 1.0 copy-start.6
  172.1 1.0 copy-start.9
  172.1 1.1 copy-start.11
  172.1 390.2 %reduce-scatter.11.cloned.1.call-start = ((), (), s32[]{:S(2)}) async-start(), calls=%async_computation.7 | async-start | bytes 110592 | tf_op jit(solution)/shard_map/reduce_scatter | solution.py:41
  173.5 402.4 %copy-start.2 = (bf16[1,128,1024]{2,1,0:T(8,128)(2,1)S(1)}, bf16[1,128,1024]{2,1,0:T(8,128)(2,1)}, u32[]{:S(2)}) copy-start(bf16[1,128,1024]{2,1,0:T(8,128)(2,1)} %copy-done.1) | copy-start | bytes 786436
  173.5 402.4 %copy-start.4 = (bf16[1,128,1024]{2,1,0:T(8,128)(2,1)S(1)}, bf16[1,128,1024]{2,1,0:T(8,128)(2,1)}, u32[]{:S(2)}) copy-start(bf16[1,128,1024]{2,1,0:T(8,128)(2,1)} %copy-done.3) | copy-start | bytes 786436
  262.1 305.1 %collective-permute-start.2 = (f32[3,8,128]{2,1,0:T(8,128)}, f32[3,8,128]{2,1,0:T(8,128)S(1)}, u32[]{:S(2)}, u32[]{:S(2)}) collective-permute-start(f32[3,8,128]{2,1,0:T(8,128)} %reduce-scatter.5.cloned.1.call-done), channel_id=1, source_target_pairs={{504,0},{0,8},{8,16},{16,24},{24,32},{32,40},{40,48},{48,56},{56,6... | collective-permute-start | bytes 36872 | tf_op jit(solution)/shard_map/ppermute | solution.py:12
  362.3 205.0 %collective-permute-start.5 = (f32[3,8,128]{2,1,0:T(8,128)}, f32[3,8,128]{2,1,0:T(8,128)S(1)}, u32[]{:S(2)}, u32[]{:S(2)}) collective-permute-start(f32[3,8,128]{2,1,0:T(8,128)} %reduce-scatter.7.cloned.1.call-done), channel_id=1, source_target_pairs={{496,0},{504,8},{0,16},{8,24},{16,32},{24,40},{32,48},{40,56},{48,... | collective-permute-start | bytes 36872 | tf_op jit(solution)/shard_map/ppermute | solution.py:12
  462.3 104.9 %collective-permute-start.8 = (f32[3,8,128]{2,1,0:T(8,128)}, f32[3,8,128]{2,1,0:T(8,128)S(1)}, u32[]{:S(2)}, u32[]{:S(2)}) collective-permute-start(f32[3,8,128]{2,1,0:T(8,128)} %reduce-scatter.9.cloned.1.call-done), channel_id=1, source_target_pairs={{488,0},{496,8},{504,16},{0,24},{8,32},{16,40},{24,48},{32,56},{40... | collective-permute-start | bytes 36872 | tf_op jit(solution)/shard_map/ppermute | solution.py:12
  562.3 13.6 %collective-permute-start.11 = (f32[3,8,128]{2,1,0:T(8,128)}, f32[3,8,128]{2,1,0:T(8,128)S(1)}, u32[]{:S(2)}, u32[]{:S(2)}) collective-permute-start(f32[3,8,128]{2,1,0:T(8,128)} %reduce-scatter.11.cloned.1.call-done), channel_id=1, source_target_pairs={{480,0},{488,8},{496,16},{504,24},{0,32},{8,40},{16,48},{24,56},{3... | collective-permute-start | bytes 36872 | tf_op jit(solution)/shard_map/ppermute | solution.py:12
Sparse Core Ops, SparseCore 0:
  165.2 96.8 reduce-scatter.4
  266.6 95.6 reduce-scatter.6
  366.7 95.5 reduce-scatter.8
  466.6 95.5 reduce-scatter.10
where the time goes:
time: 586 us; the launch traced here: 583 us
  waiting for transfers between devices  382 us (65%)
  blocking collectives  113 us (19%)
  starting transfers between devices  61.2 us (10%)
  between operations  13.5 us (2%)
  other arithmetic  8.01 us (1%)
    reduce_scatter x4, waiting for transfers between devices, body(): lax.psum_scatter(mirror_terms, 'tile', scatter_dimension=2, tiled=True)  373 us
    ppermute x12, starting transfers between devices, from_behind(): return lax.ppermute(block, axis, route)  61 us
    all_gather x1, blocking collectives, body(): group_pts = lax.all_gather(points, 'tile', axis=1, tiled=True)  58.8 us
    all_gather x1, blocking collectives, body(): group_probe = lax.all_gather(probes, 'tile', axis=1, tiled=True)  54 us
  transfers between devices with their start and end apart: 16, of which 5 were waited for; matrix products, arithmetic and copies ran while one was open for 2% of the time, Pallas kernels for 0%

commit v1 on v0

v1 whole, which is shorter than its diff:
```python
import math

import jax
import jax.numpy as jnp
import numpy as np
from jax import lax
from jax.experimental import pallas as pl
from jax.experimental.pallas import tpu as pltpu
from jax.sharding import PartitionSpec as P

ROUNDS = 4
PLANE_GROUPS = 8
PLANES = 16
ROW_TILES = 4
LANES = 128
ROW_CHUNK = 16
COL_CHUNK = 256
SCALES = np.array([[math.sqrt(3) / 0.35], [math.sqrt(3) / 0.35], [math.sqrt(3) / 0.25]], np.float32)


def device_at(plane, member, column):
    return ((plane % 8) * PLANE_GROUPS + member) * 8 + (plane // 8) * ROW_TILES + column


def next_plane(block):
    route = []
    for plane in range(PLANES):
        for member in range(PLANE_GROUPS):
            step = -1 if member < PLANE_GROUPS // 2 else 1
            for column in range(ROW_TILES):
                route.append(
                    (
                        device_at(plane, member, column),
                        device_at((plane + step) % PLANES, member, column),
                    )
                )
    return lax.ppermute(block, ("grp", "tile"), route)


def other_half(block):
    return lax.ppermute(block, "tile", [(i, i ^ 4) for i in range(8)])


def within_plane(block):
    planes = [
        [device_at(plane, m, c) for m in range(PLANE_GROUPS) for c in range(ROW_TILES)]
        for plane in range(PLANES)
    ]
    copies = jnp.broadcast_to(block[None], (len(planes[0]),) + block.shape)
    return lax.all_to_all(copies, ("grp", "tile"), 0, 0, axis_index_groups=planes)


def pack(points, probes):
    scaled = (points - 2.0) * SCALES
    lead = lax.reduce_precision(scaled, 8, 7)
    rest = scaled - lead
    unused = jnp.zeros((2, points.shape[1]), jnp.bfloat16)
    return jnp.concatenate(
        [probes, lead.astype(jnp.bfloat16), rest.astype(jnp.bfloat16), unused], 0
    )


def products_kernel(own_ref, far_ref, out_ref, rows_ref, tile_ref):
    own = own_ref[...].astype(jnp.float32)
    coords = jnp.concatenate([own[8:11] + own[11:14], jnp.zeros((5, LANES), jnp.float32)], 0)
    upright = jnp.transpose(coords)
    for k in range(3):
        rows_ref[k] = jnp.broadcast_to(upright[:, k : k + 1], (LANES, LANES))
    member = lax.rem(lax.axis_index("grp"), PLANE_GROUPS)
    blocks = COL_CHUNK // LANES

    def tiles(cols, at):
        parts = []
        for col in cols:
            d = [rows_ref[k, pl.ds(at, ROW_CHUNK), :] - col[k] for k in range(3)]
            flat_q = d[0] * d[0] + d[1] * d[1]
            depth_q = d[2] * d[2]
            total = (flat_q + depth_q) + 1e-6
            scaled = total * lax.rsqrt(total)
            decay = jnp.exp2(math.log2(1.3) - scaled * math.log2(math.e))
            parts.append(((1.0 + scaled) * decay, flat_q * decay, depth_q * decay))
        return [jnp.concatenate([p[k] for p in parts], 1).astype(jnp.bfloat16) for k in range(3)]

    def step(n, total):
        at = member + jnp.where(n < ROUNDS, n - ROUNDS, n - ROUNDS + 1)
        sender = lax.rem(at + PLANE_GROUPS, PLANE_GROUPS)
        kind = jnp.where((at >= 0) & (at < PLANE_GROUPS), 0, 1)
        for half in range(2):
            for part in range(ROW_TILES // blocks):
                cells = [
                    far_ref[sender * ROW_TILES + part * blocks + w, half * 2 + kind]
                    for w in range(blocks)
                ]
                probe = jnp.concatenate([cell[0:8] for cell in cells], 1)
                wide = [cell.astype(jnp.float32) for cell in cells]
                cols = [
                    [
                        jnp.broadcast_to(f[8 + k : 9 + k] + f[11 + k : 12 + k], (ROW_CHUNK, LANES))
                        for k in range(3)
                    ]
                    for f in wide
                ]
                slot = half * 2 + part
                for start in range(0, LANES, ROW_CHUNK):
                    made = tiles(cols, start)
                    for k in range(3):
                        tile_ref[slot, pl.ds(k * LANES + start, ROW_CHUNK), :] = made[k]
                total = total + lax.dot_general(
                    probe,
                    tile_ref[slot],
                    (((1,), (1,)), ((), ())),
                    preferred_element_type=jnp.float32,
                )
        return total

    total = lax.fori_loop(0, 2 * ROUNDS, step, jnp.zeros((8, 3 * LANES), jnp.float32))
    for k in range(3):
        out_ref[k] = total[:, k * LANES : (k + 1) * LANES]


def products(own, far):
    return pl.pallas_call(
        products_kernel,
        out_shape=jax.ShapeDtypeStruct((3, 8, LANES), jnp.float32),
        in_specs=[pl.BlockSpec(memory_space=pltpu.VMEM)] * 2,
        out_specs=pl.BlockSpec(memory_space=pltpu.VMEM),
        scratch_shapes=[
            pltpu.VMEM((3, LANES, LANES), jnp.float32),
            pltpu.VMEM((4, 3 * LANES, COL_CHUNK), jnp.bfloat16),
        ],
        compiler_params=pltpu.CompilerParams(vmem_limit_bytes=32 * 2**20),
    )(own, far)


def body(points, probes):
    own = pack(points, probes)
    held = jnp.stack([own, next_plane(own)])
    held = jnp.concatenate([held, other_half(held)], 0)
    return products(own, within_plane(held))


def solution(mesh):
    return jax.shard_map(
        body,
        mesh=mesh,
        in_specs=(P(None, ("grp", "tile")), P(None, ("grp", "tile"))),
        out_specs=P(None, None, ("grp", "tile")),
        check_vma=False,
    )
```

time: 586 us -> 53.9 us (0.09)
  waiting for transfers between devices: 382 us -> 5.83 us
  blocking collectives: 113 us -> 21.2 us
  starting transfers between devices: 61.2 us -> 19.9 us
  between operations: 13.5 us -> 0.04 us
  other arithmetic: 8.01 us -> 0.23 us
    reduce_scatter x4 -> x0, waiting for transfers between devices: 373 us -> none  [body(): lax.psum_scatter(mirror_terms, 'tile', scatter_dimension=2, tiled=True)]
    all_gather x2 -> x0, blocking collectives: 113 us -> none  [the longest x1 58.8 us: body(): group_pts = lax.all_gather(points, 'tile', axis=1, tiled=True)]
    ppermute x12 -> x2, starting transfers between devices: 61 us -> 19.9 us  [the longest x1 11.9 us: next_plane(): return lax.ppermute(block, ('grp', 'tile'), route)]
    all_to_all x0 -> x1, blocking collectives: none -> 21.2 us  [within_plane(): lax.all_to_all(copies, ('grp', 'tile'), 0, 0, axis_index_groups=planes)]
  transfers between devices with their start and end apart: 16 -> 2, of which waited for: 5 -> 2; matrix products, arithmetic and copies ran while one was open for 2% -> 0% of each run, Pallas kernels for 0% -> 0%
where the time goes in v1:
time: 53.9 us; the launch traced here: 53.6 us
  blocking collectives  21.2 us (39%)
  starting transfers between devices  19.9 us (37%)
  waiting for transfers between devices  5.83 us (11%)
  Pallas kernels  5 us (9%)
  local copies, waits for them, and re-layouts  1.47 us (3%)
    all_to_all x1, blocking collectives, within_plane(): lax.all_to_all(copies, ('grp', 'tile'), 0, 0, axis_index_groups=planes)  21.2 us
    ppermute x1, starting transfers between devices, next_plane(): return lax.ppermute(block, ('grp', 'tile'), route)  11.9 us
    ppermute x1, starting transfers between devices, other_half(): return lax.ppermute(block, 'tile', [(i, i ^ 4) for i in range(8)])  7.92 us
    ppermute x1, waiting for transfers between devices, other_half(): return lax.ppermute(block, 'tile', [(i, i ^ 4) for i in range(8)])  5.17 us
    pallas_call x1, Pallas kernels, products(): pl.pallas_call(products_kernel, out_shape=jax.ShapeDtypeStruct((3, 8, LAN...  5 us
    unnamed x6, local copies, waits for them, and re-layouts  1.28 us
  transfers between devices with their start and end apart: 2, of which 2 were waited for; matrix products, arithmetic and copies ran while one was open for 0% of the time, Pallas kernels for 0%

profile of v1, /device:TPU:1, one launch (start us, length us, event | category | flops | bytes accessed | tf_op | source)
XLA Modules:
  0.0 53.6 jit_solution(8591137428968808519)
XLA Ops:
  0.0 0.0 copy-start.1
  0.0 0.0 copy-start.2
  0.0 0.1 pad.8.clone
  0.1 0.6 %copy-done.1 = f32[3,128]{1,0:T(4,128)S(1)} copy-done((f32[3,128]{1,0:T(4,128)S(1)}, f32[3,128]{1,0:T(4,128)}, u32[]{:S(2)}) %copy-start.1) | copy-done | bytes 1560
  0.7 0.0 copy-done.2
  0.7 0.1 reduce-precision_convert_fusion
  0.8 0.0 copy-start
  0.8 0.7 %copy-done = bf16[8,128]{1,0:T(8,128)(2,1)S(1)} copy-done((bf16[8,128]{1,0:T(8,128)(2,1)S(1)}, bf16[8,128]{1,0:T(8,128)(2,1)}, u32[]{:S(2)}) %copy-start) | copy-done | bytes 2072
  1.4 0.1 maximum_maximum_fusion.own_ref
  1.5 11.9 %collective-permute-start = (bf16[16,128]{1,0:T(8,128)(2,1)S(1)}, bf16[16,128]{1,0:T(8,128)(2,1)S(1)}, u32[]{:S(2)}, u32[]{:S(2)}) collective-permute-start(bf16[16,128]{1,0:T(8,128)(2,1)S(1)} %maximum_maximum_fusion.own_ref), channel_id=1, source_target_pairs={{0,452},{1,453},{2,454},{3,455},{8,460},{9,461},{10,462},{11,463},... | collective-permute-start | bytes 12296 | tf_op jit(solution)/shard_map/ppermute | solution.py:37
  13.5 0.1 fusion.1
  13.5 0.7 %collective-permute-done = bf16[16,128]{1,0:T(8,128)(2,1)S(1)} collective-permute-done((bf16[16,128]{1,0:T(8,128)(2,1)S(1)}, bf16[16,128]{1,0:T(8,128)(2,1)S(1)}, u32[]{:S(2)}, u32[]{:S(2)}) %collective-permute-start) | collective-permute-done | bytes 4128 | tf_op jit(solution)/shard_map/ppermute | solution.py:37
  14.2 7.9 %collective-permute-start.1 = (bf16[2,16,128]{2,1,0:T(8,128)(2,1)S(1)}, bf16[2,16,128]{2,1,0:T(8,128)(2,1)S(1)}, u32[]{:S(2)}, u32[]{:S(2)}) collective-permute-start(bf16[2,16,128]{2,1,0:T(8,128)(2,1)S(1)} %pad_maximum_fusion.1), channel_id=1, source_target_pairs={{0,4},{1,5},{2,6},{3,7},{4,0},{5,1},{6,2},{7,3},{8,12},{9,13},{10,... | collective-permute-start | bytes 24584 | tf_op jit(solution)/shard_map/ppermute | solution.py:41
  22.1 5.2 %collective-permute-done.1 = bf16[2,16,128]{2,1,0:T(8,128)(2,1)S(1)} collective-permute-done((bf16[2,16,128]{2,1,0:T(8,128)(2,1)S(1)}, bf16[2,16,128]{2,1,0:T(8,128)(2,1)S(1)}, u32[]{:S(2)}, u32[]{:S(2)}) %collective-permute-start.1) | collective-permute-done | bytes 8224 | tf_op jit(solution)/shard_map/ppermute | solution.py:41
  27.3 0.1 broadcast_in_dim.10
  27.4 21.2 %all_to_all.5.far_ref = bf16[32,4,16,128]{3,2,1,0:T(8,128)(2,1)S(1)} all-to-all(bf16[32,4,16,128]{3,2,1,0:T(8,128)(2,1)S(1)} %broadcast_in_dim.10), channel_id=1, replica_groups={{0,1,2,3,8,9,10,11,16,17,18,19,24,25,26,27,32,33,34,35,40,41,42,43,48,4..., dimensions={0} | all-to-all | bytes 1048576 | tf_op jit(solution)/shard_map/all_to_all | solution.py:50
  48.6 5.0 %shard_map.37 = f32[3,8,128]{2,1,0:T(8,128)} custom-call(bf16[16,128]{1,0:T(8,128)(2,1)S(1)} %maximum_maximum_fusion.own_ref, bf16[32,4,16,128]{3,2,1,0:T(8,128)(2,1)S(1)} %all_to_all.5.far_ref), custom_call_target="tpu_custom_call" | custom-call | tf_op jit(solution)/shard_map/pallas_call | solution.py:122
  (3 shorter events, 0.0 us)
Async XLA Ops:
  0.0 0.7 %copy-start.1 = (f32[3,128]{1,0:T(4,128)S(1)}, f32[3,128]{1,0:T(4,128)}, u32[]{:S(2)}) copy-start(f32[3,128]{1,0:T(4,128)} %param.3) | copy-start | bytes 4612
  0.0 0.7 %copy-start.2 = (f32[3]{0:T(128)S(1)}, f32[3]{0:T(128)}, u32[]{:S(2)}) copy-start(f32[3]{0:T(128)} %constant.10) | copy-start | bytes 40
  0.8 0.7 %copy-start = (bf16[8,128]{1,0:T(8,128)(2,1)S(1)}, bf16[8,128]{1,0:T(8,128)(2,1)}, u32[]{:S(2)}) copy-start(bf16[8,128]{1,0:T(8,128)(2,1)} %param.4) | copy-start | bytes 6148
  1.5 12.7 %collective-permute-start = (bf16[16,128]{1,0:T(8,128)(2,1)S(1)}, bf16[16,128]{1,0:T(8,128)(2,1)S(1)}, u32[]{:S(2)}, u32[]{:S(2)}) collective-permute-start(bf16[16,128]{1,0:T(8,128)(2,1)S(1)} %maximum_maximum_fusion.own_ref), channel_id=1, source_target_pairs={{0,452},{1,453},{2,454},{3,455},{8,460},{9,461},{10,462},{11,463},... | collective-permute-start | bytes 12296 | tf_op jit(solution)/shard_map/ppermute | solution.py:37
  14.2 13.1 %collective-permute-start.1 = (bf16[2,16,128]{2,1,0:T(8,128)(2,1)S(1)}, bf16[2,16,128]{2,1,0:T(8,128)(2,1)S(1)}, u32[]{:S(2)}, u32[]{:S(2)}) collective-permute-start(bf16[2,16,128]{2,1,0:T(8,128)(2,1)S(1)} %pad_maximum_fusion.1), channel_id=1, source_target_pairs={{0,4},{1,5},{2,6},{3,7},{4,0},{5,1},{6,2},{7,3},{8,12},{9,13},{10,... | collective-permute-start | bytes 24584 | tf_op jit(solution)/shard_map/ppermute | solution.py:41

commit v2 on v1

v2 whole, which is shorter than its diff:
```python
import math

import jax
import jax.numpy as jnp
from jax import lax
from jax.experimental import pallas as pl
from jax.experimental.pallas import tpu as pltpu
from jax.sharding import PartitionSpec as P

ROUNDS = 4
PLANE_GROUPS = 8
PLANES = 16
ROW_TILES = 4
LANES = 128
ROWS = 24
ROW_CHUNK = 16
COL_CHUNK = 256
SCALES = (math.sqrt(3) / 0.35, math.sqrt(3) / 0.35, math.sqrt(3) / 0.25)


def device_at(plane, member, column):
    return ((plane % 8) * PLANE_GROUPS + member) * 8 + (plane // 8) * ROW_TILES + column


def across_planes(block):
    sets = []
    for plane in range(PLANES // 2):
        for member in range(4, PLANE_GROUPS):
            for column in range(ROW_TILES):
                lower = (member + 2) % 4
                near = [device_at(plane, member, column), device_at(plane + 1, lower, column)]
                far = [
                    device_at(plane + 8, member, column),
                    device_at((plane + 9) % PLANES, lower, column),
                ]
                sets.append(near + far if plane == 7 else far + near)
    copies = jnp.broadcast_to(block[None], (4,) + block.shape)
    return lax.all_to_all(copies, ("grp", "tile"), 0, 0, axis_index_groups=sets)


def within_plane(block):
    planes = [
        [
            device_at(plane, 2 * m + core, c)
            for m in reversed(range(PLANE_GROUPS // 2))
            for c in reversed(range(ROW_TILES))
        ]
        for plane in range(PLANES)
        for core in range(2)
    ]
    copies = jnp.broadcast_to(block[None], (len(planes[0]),) + block.shape)
    return lax.all_to_all(copies, ("grp", "tile"), 0, 0, axis_index_groups=planes)


def other_core(block):
    return lax.ppermute(block, "grp", [(i, i ^ 1) for i in range(64)])


def pack_kernel(points_ref, probes_ref, out_ref):
    rest = points_ref[...]
    parts = []
    for _ in range(3):
        part = rest.astype(jnp.bfloat16).astype(jnp.float32)
        parts += [part, jnp.zeros((1, LANES), jnp.float32)]
        rest = rest - part
    probes = probes_ref[...].astype(jnp.float32)
    out_ref[...] = jnp.concatenate(
        [probes] + parts + [jnp.zeros((4, LANES), jnp.float32)], 0
    ).astype(jnp.bfloat16)


def pack(points, probes):
    return pl.pallas_call(
        pack_kernel,
        out_shape=jax.ShapeDtypeStruct((ROWS, LANES), jnp.bfloat16),
        in_specs=[pl.BlockSpec(memory_space=pltpu.VMEM)] * 2,
        out_specs=pl.BlockSpec(memory_space=pltpu.VMEM),
    )(points, probes)


def unpack(block):
    wide = block.astype(jnp.float32)
    return wide[0:8], (wide[8:11] + wide[12:15]) + wide[16:19]


def products_kernel(first, *refs):
    if first:
        own_ref, far_ref, out_ref, rows_ref, tile_ref = refs
    else:
        own_ref, far_ref, before_ref, out_ref, rows_ref, tile_ref = refs
    own = unpack(own_ref[...])[1]
    centre = own[:, 0:1]
    upright = jnp.transpose(jnp.concatenate([own, jnp.zeros((5, LANES), jnp.float32)], 0))
    for k in range(3):
        column = (upright[:, k : k + 1] - centre[k : k + 1]) * SCALES[k]
        rows_ref[k] = jnp.broadcast_to(column, (LANES, LANES))
    member = lax.rem(lax.axis_index("grp"), PLANE_GROUPS)
    blocks = COL_CHUNK // LANES

    def tiles(cols, at):
        parts = []
        for col in cols:
            d = [rows_ref[k, pl.ds(at, ROW_CHUNK), :] - col[k] for k in range(3)]
            flat_q = d[0] * d[0] + d[1] * d[1]
            depth_q = d[2] * d[2]
            total = (flat_q + depth_q) + 1e-6
            scaled = total * lax.rsqrt(total)
            decay = jnp.exp2(math.log2(1.3) - scaled * math.log2(math.e))
            parts.append(((1.0 + scaled) * decay, flat_q * decay, depth_q * decay))
        return [jnp.concatenate([p[k] for p in parts], 1).astype(jnp.bfloat16) for k in range(3)]

    if first:
        total = jnp.zeros((8, 3 * LANES), jnp.float32)
    else:
        total = jnp.concatenate([before_ref[k] for k in range(3)], 1)
    slot = 0
    for offset in (-4, -2, 2, 4) if first else (-3, -1, 1, 3):
        wanted = member + offset
        group = lax.rem(wanted + PLANE_GROUPS, PLANE_GROUPS)
        inside = (wanted >= 0) & (wanted < PLANE_GROUPS)
        twin = lax.rem(group + 2, 4) + jnp.where(group < 4, 4, 0)
        place = (PLANE_GROUPS - 1 - jnp.where(inside, group, twin)) // 2
        kind = jnp.where(group < 4, 1, 0)
        for half in range(2):
            for part in range(ROW_TILES // blocks):
                cells = [
                    unpack(far_ref[place * ROW_TILES + part * blocks + w, 2 * half + kind])
                    for w in range(blocks)
                ]
                probe = jnp.concatenate([cell[0] for cell in cells], 1).astype(jnp.bfloat16)
                cols = [
                    [
                        jnp.broadcast_to(
                            (cell[1][k : k + 1] - centre[k : k + 1]) * SCALES[k],
                            (ROW_CHUNK, LANES),
                        )
                        for k in range(3)
                    ]
                    for cell in cells
                ]
                for start in range(0, LANES, ROW_CHUNK):
                    made = tiles(cols, start)
                    for k in range(3):
                        tile_ref[slot % 4, pl.ds(k * LANES + start, ROW_CHUNK), :] = made[k]
                total = total + lax.dot_general(
                    probe,
                    tile_ref[slot % 4],
                    (((1,), (1,)), ((), ())),
                    preferred_element_type=jnp.float32,
                )
                slot += 1
    for k in range(3):
        out_ref[k] = total[:, k * LANES : (k + 1) * LANES]


def products(own, far, before=None):
    operands = (own, far) if before is None else (own, far, before)
    return pl.pallas_call(
        lambda *refs: products_kernel(before is None, *refs),
        out_shape=jax.ShapeDtypeStruct((3, 8, LANES), jnp.float32),
        in_specs=[pl.BlockSpec(memory_space=pltpu.VMEM)] * len(operands),
        out_specs=pl.BlockSpec(memory_space=pltpu.VMEM),
        scratch_shapes=[
            pltpu.VMEM((3, LANES, LANES), jnp.float32),
            pltpu.VMEM((4, 3 * LANES, COL_CHUNK), jnp.bfloat16),
        ],
        compiler_params=pltpu.CompilerParams(vmem_limit_bytes=32 * 2**20),
        cost_estimate=pl.CostEstimate(flops=30_000_000, bytes_accessed=500_000, transcendentals=1_000_000),
    )(*operands)


def body(points, probes):
    own = pack(points, probes)
    same = within_plane(across_planes(own))
    swapped = other_core(same)
    return products(own, swapped, products(own, same))


def solution(mesh):
    return jax.shard_map(
        body,
        mesh=mesh,
        in_specs=(P(None, ("grp", "tile")), P(None, ("grp", "tile"))),
        out_specs=P(None, None, ("grp", "tile")),
        check_vma=False,
    )
```

time: 53.9 us -> 48.2 us (0.89)
  blocking collectives: 21.2 us -> 36.8 us
  starting transfers between devices: 19.9 us -> 4.93 us
  waiting for transfers between devices: 5.83 us -> 0.01 us
  local copies, waits for them, and re-layouts: 1.47 us -> 0.75 us
    all_to_all x0 -> x1, blocking collectives: none -> 25.2 us  [across_planes(): return lax.all_to_all(copies, ('grp', 'tile'), 0, 0, axis_index_groups=sets)]
    ppermute x2 -> x1, starting transfers between devices: 19.9 us -> 4.93 us  [other_core(): return lax.ppermute(block, 'grp', [(i, i ^ 1) for i in range(64)])]
    all_to_all x1, blocking collectives: 21.2 us -> 11.5 us  [within_plane(): lax.all_to_all(copies, ('grp', 'tile'), 0, 0, axis_index_groups=planes)]
    ppermute x2 -> x1, waiting for transfers between devices: 5.83 us -> 0.01 us  [other_core(): return lax.ppermute(block, 'grp', [(i, i ^ 1) for i in range(64)])]
    unnamed x6 -> x2, local copies, waits for them, and re-layouts: 1.28 us -> 0.01 us
    broadcast_in_dim x1, local copies, waits for them, and re-layouts: 0.01 us -> 0.69 us  [across_planes(): copies = jnp.broadcast_to(block[None], (4,) + block.shape)]
    pallas_call x1 -> x3, Pallas kernels: 5 us -> 5.45 us  [the longest x2 4.15 us: products(): pl.pallas_call(lambda *refs: products_kernel(before is None, *refs), out_...]
  transfers between devices with their start and end apart: 2 -> 1, of which waited for: 2 -> 0; matrix products, arithmetic and copies ran while one was open for 0% -> 0% of each run, Pallas kernels for 0% -> 4%
where the time goes in v2:
time: 48.2 us; the launch traced here: 48 us
  blocking collectives  36.8 us (76%)
  Pallas kernels  5.45 us (11%)
  starting transfers between devices  4.93 us (10%)
  local copies, waits for them, and re-layouts  0.75 us (2%)
    all_to_all x1, blocking collectives, across_planes(): return lax.all_to_all(copies, ('grp', 'tile'), 0, 0, axis_index_groups=sets)  25.2 us
    all_to_all x1, blocking collectives, within_plane(): lax.all_to_all(copies, ('grp', 'tile'), 0, 0, axis_index_groups=planes)  11.5 us
    ppermute x1, starting transfers between devices, other_core(): return lax.ppermute(block, 'grp', [(i, i ^ 1) for i in range(64)])  4.93 us
    pallas_call x2, Pallas kernels, products(): pl.pallas_call(lambda *refs: products_kernel(before is None, *refs), out_...  4.15 us
    pallas_call x1, Pallas kernels, pack(): pl.pallas_call(pack_kernel, out_shape=jax.ShapeDtypeStruct((ROWS, LANES),...  1.3 us
  transfers between devices with their start and end apart: 1, of which 0 were waited for; matrix products, arithmetic and copies ran while one was open for 0% of the time, Pallas kernels for 4%

profile of v2, /device:TPU:1, one launch (start us, length us, event | category | flops | bytes accessed | tf_op | source)
XLA Modules:
  0.0 48.0 jit_solution(17165523091274965050)
XLA Ops:
  0.0 1.3 %shard_map.28.refs_0_ = bf16[24,128]{1,0:T(8,128)(2,1)} custom-call(f32[3,128]{1,0:T(4,128)} %points_ref.1, bf16[8,128]{1,0:T(8,128)(2,1)} %probes_ref.1), custom_call_target="tpu_custom_call" | custom-call | tf_op jit(solution)/shard_map/pallas_call | solution.py:73
  1.3 0.7 %broadcast_in_dim.4 = bf16[4,24,128]{2,1,0:T(8,128)(2,1)S(1)} broadcast(bf16[24,128]{1,0:T(8,128)(2,1)} %shard_map.28.refs_0_), dimensions={1,2} | broadcast | bytes 30720 | tf_op jit(solution)/shard_map/broadcast_in_dim | solution.py:37
  2.0 25.2 %all_to_all.10 = bf16[4,24,128]{2,1,0:T(8,128)(2,1)S(1)} all-to-all(bf16[4,24,128]{2,1,0:T(8,128)(2,1)S(1)} %broadcast_in_dim.4), channel_id=1, replica_groups={{36,84,32,80},{37,85,33,81},{38,86,34,82},{39,87,35,83},{44,92,40,88},{..., dimensions={0} | all-to-all | bytes 49152 | tf_op jit(solution)/shard_map/all_to_all | solution.py:38
  27.2 0.1 broadcast_in_dim.5
  27.3 0.0 copy-start
  27.3 11.5 %all_to_all.11.refs_1_ = bf16[16,4,24,128]{3,2,1,0:T(8,128)(2,1)S(1)} all-to-all(bf16[16,4,24,128]{3,2,1,0:T(8,128)(2,1)S(1)} %broadcast_in_dim.5), channel_id=1, replica_groups={{51,50,49,48,35,34,33,32,19,18,17,16,3,2,1,0},{59,58,57,56,43,42,41,40,..., dimensions={0} | all-to-all | bytes 786432 | tf_op jit(solution)/shard_map/all_to_all | solution.py:52
  38.8 4.9 %collective-permute-start = (bf16[16,4,24,128]{3,2,1,0:T(8,128)(2,1)S(1)}, bf16[16,4,24,128]{3,2,1,0:T(8,128)(2,1)S(1)}, u32[]{:S(2)}, u32[]{:S(2)}) collective-permute-start(bf16[16,4,24,128]{3,2,1,0:T(8,128)(2,1)S(1)} %all_to_all.11.refs_1_), channel_id=1, source_target_pairs={{0,8},{8,0},{16,24},{24,16},{32,40},{40,32},{48,56},{56,48},{64,72... | collective-permute-start | bytes 1179656 | tf_op jit(solution)/shard_map/ppermute | solution.py:56
  43.8 0.0 copy-done
  43.8 1.7 %shard_map.29.refs_2_ = f32[3,8,128]{2,1,0:T(8,128)S(1)} custom-call(bf16[24,128]{1,0:T(8,128)(2,1)S(1)} %copy-done, bf16[16,4,24,128]{3,2,1,0:T(8,128)(2,1)S(1)} %all_to_all.11.refs_1_), custom_call_target="tpu_custom_call" | custom-call | flops 30000000 | bytes 500000 | tf_op jit(solution)/shard_map/pallas_call | solution.py:158
  45.5 0.0 collective-permute-done.refs_1_
  45.5 2.4 %shard_map.30 = f32[3,8,128]{2,1,0:T(8,128)} custom-call(bf16[24,128]{1,0:T(8,128)(2,1)S(1)} %copy-done, bf16[16,4,24,128]{3,2,1,0:T(8,128)(2,1)S(1)} %collective-permute-done.refs_1_, f32[3,8,128]{2,1,0:T(8,128)S(1)} %shard_map.29.refs_2_), custom_call_target="tpu_custom_call" | custom-call | flops 30000000 | bytes 500000 | tf_op jit(solution)/shard_map/pallas_call | solution.py:158
Async XLA Ops:
  27.3 16.5 %copy-start = (bf16[24,128]{1,0:T(8,128)(2,1)S(1)}, bf16[24,128]{1,0:T(8,128)(2,1)}, u32[]{:S(2)}) copy-start(bf16[24,128]{1,0:T(8,128)(2,1)} %shard_map.28.refs_0_) | copy-start | bytes 18436
  38.8 6.7 %collective-permute-start = (bf16[16,4,24,128]{3,2,1,0:T(8,128)(2,1)S(1)}, bf16[16,4,24,128]{3,2,1,0:T(8,128)(2,1)S(1)}, u32[]{:S(2)}, u32[]{:S(2)}) collective-permute-start(bf16[16,4,24,128]{3,2,1,0:T(8,128)(2,1)S(1)} %all_to_all.11.refs_1_), channel_id=1, source_target_pairs={{0,8},{8,0},{16,24},{24,16},{32,40},{40,32},{48,56},{56,48},{64,72... | collective-permute-start | bytes 1179656 | tf_op jit(solution)/shard_map/ppermute | solution.py:56

commit v3 on v2

--- a/solution.py
+++ b/solution.py
@@ -22,7 +22,7 @@
     return ((plane % 8) * PLANE_GROUPS + member) * 8 + (plane // 8) * ROW_TILES + column
 
 
-def across_planes(block):
+def across_planes(copies):
     sets = []
     for plane in range(PLANES // 2):
         for member in range(4, PLANE_GROUPS):
@@ -34,7 +34,6 @@
                     device_at((plane + 9) % PLANES, lower, column),
                 ]
                 sets.append(near + far if plane == 7 else far + near)
-    copies = jnp.broadcast_to(block[None], (4,) + block.shape)
     return lax.all_to_all(copies, ("grp", "tile"), 0, 0, axis_index_groups=sets)
 
 
@@ -42,8 +41,8 @@
     planes = [
         [
             device_at(plane, 2 * m + core, c)
-            for m in reversed(range(PLANE_GROUPS // 2))
-            for c in reversed(range(ROW_TILES))
+            for m in range(PLANE_GROUPS // 2)
+            for c in (2, 3, 0, 1)
         ]
         for plane in range(PLANES)
         for core in range(2)
@@ -64,17 +63,22 @@
         parts += [part, jnp.zeros((1, LANES), jnp.float32)]
         rest = rest - part
     probes = probes_ref[...].astype(jnp.float32)
-    out_ref[...] = jnp.concatenate(
+    packed = jnp.concatenate(
         [probes] + parts + [jnp.zeros((4, LANES), jnp.float32)], 0
     ).astype(jnp.bfloat16)
+    for copy in range(4):
+        out_ref[copy] = packed
 
 
 def pack(points, probes):
+    points = pltpu.with_memory_space_constraint(points, pltpu.HBM)
+    probes = pltpu.with_memory_space_constraint(probes, pltpu.HBM)
     return pl.pallas_call(
         pack_kernel,
-        out_shape=jax.ShapeDtypeStruct((ROWS, LANES), jnp.bfloat16),
+        out_shape=jax.ShapeDtypeStruct((4, ROWS, LANES), jnp.bfloat16),
         in_specs=[pl.BlockSpec(memory_space=pltpu.VMEM)] * 2,
         out_specs=pl.BlockSpec(memory_space=pltpu.VMEM),
+        compiler_params=pltpu.CompilerParams(vmem_limit_bytes=2**20),
     )(points, probes)
 
 
@@ -88,7 +92,7 @@
         own_ref, far_ref, out_ref, rows_ref, tile_ref = refs
     else:
         own_ref, far_ref, before_ref, out_ref, rows_ref, tile_ref = refs
-    own = unpack(own_ref[...])[1]
+    own = unpack(own_ref[0])[1]
     centre = own[:, 0:1]
     upright = jnp.transpose(jnp.concatenate([own, jnp.zeros((5, LANES), jnp.float32)], 0))
     for k in range(3):
@@ -119,7 +123,7 @@
         group = lax.rem(wanted + PLANE_GROUPS, PLANE_GROUPS)
         inside = (wanted >= 0) & (wanted < PLANE_GROUPS)
         twin = lax.rem(group + 2, 4) + jnp.where(group < 4, 4, 0)
-        place = (PLANE_GROUPS - 1 - jnp.where(inside, group, twin)) // 2
+        place = jnp.where(inside, group, twin) // 2
         kind = jnp.where(group < 4, 1, 0)
         for half in range(2):
             for part in range(ROW_TILES // blocks):

time: 48.2 us -> 46.5 us (0.965)
  local copies, waits for them, and re-layouts: 0.75 us -> 0.05 us
  Pallas kernels: 5.45 us -> 4.87 us
    broadcast_in_dim x1 -> x0, local copies, waits for them, and re-layouts: 0.69 us -> none  [across_planes(): copies = jnp.broadcast_to(block[None], (4,) + block.shape)]
    pallas_call x1, Pallas kernels: 1.3 us -> 0.71 us  [pack(): pl.pallas_call(pack_kernel, out_shape=jax.ShapeDtypeStruct((4, ROWS, LANE...]
where the time goes in v3:
time: 46.5 us; the launch traced here: 46.3 us
  blocking collectives  36.7 us (79%)
  Pallas kernels  4.87 us (10%)
  starting transfers between devices  4.63 us (10%)
    all_to_all x1, blocking collectives, across_planes(): return lax.all_to_all(copies, ('grp', 'tile'), 0, 0, axis_index_groups=sets)  25.2 us
    all_to_all x1, blocking collectives, within_plane(): lax.all_to_all(copies, ('grp', 'tile'), 0, 0, axis_index_groups=planes)  11.5 us
    ppermute x1, starting transfers between devices, other_core(): return lax.ppermute(block, 'grp', [(i, i ^ 1) for i in range(64)])  4.63 us
    pallas_call x2, Pallas kernels, products(): pl.pallas_call(lambda *refs: products_kernel(before is None, *refs), out_...  4.16 us
  transfers between devices with their start and end apart: 1, of which 0 were waited for; matrix products, arithmetic and copies ran while one was open for 0% of the time, Pallas kernels for 4%

profile of v3, /device:TPU:1, one launch (start us, length us, event | category | flops | bytes accessed | tf_op | source)
XLA Modules:
  0.0 46.3 jit_solution(16357744920569089220)
XLA Ops:
  0.0 0.7 %shard_map.28.refs_0_ = bf16[4,24,128]{2,1,0:T(8,128)(2,1)S(1)} custom-call(f32[3,128]{1,0:T(4,128)} %points_ref.1, bf16[8,128]{1,0:T(8,128)(2,1)} %probes_ref.1), custom_call_target="tpu_custom_call" | custom-call | tf_op jit(solution)/shard_map/pallas_call | solution.py:76
  0.7 25.2 %all_to_all.10 = bf16[4,24,128]{2,1,0:T(8,128)(2,1)S(1)} all-to-all(bf16[4,24,128]{2,1,0:T(8,128)(2,1)S(1)} %shard_map.28.refs_0_), channel_id=1, replica_groups={{36,84,32,80},{37,85,33,81},{38,86,34,82},{39,87,35,83},{44,92,40,88},{..., dimensions={0} | all-to-all | bytes 49152 | tf_op jit(solution)/shard_map/all_to_all | solution.py:37
  26.0 0.1 broadcast_in_dim.2
  26.0 11.5 %all_to_all.11.refs_1_ = bf16[16,4,24,128]{3,2,1,0:T(8,128)(2,1)S(1)} all-to-all(bf16[16,4,24,128]{3,2,1,0:T(8,128)(2,1)S(1)} %broadcast_in_dim.2), channel_id=1, replica_groups={{2,3,0,1,18,19,16,17,34,35,32,33,50,51,48,49},{10,11,8,9,26,27,24,25,42..., dimensions={0} | all-to-all | bytes 786432 | tf_op jit(solution)/shard_map/all_to_all | solution.py:51
  37.5 4.6 %collective-permute-start = (bf16[16,4,24,128]{3,2,1,0:T(8,128)(2,1)S(1)}, bf16[16,4,24,128]{3,2,1,0:T(8,128)(2,1)S(1)}, u32[]{:S(2)}, u32[]{:S(2)}) collective-permute-start(bf16[16,4,24,128]{3,2,1,0:T(8,128)(2,1)S(1)} %all_to_all.11.refs_1_), channel_id=1, source_target_pairs={{0,8},{8,0},{16,24},{24,16},{32,40},{40,32},{48,56},{56,48},{64,72... | collective-permute-start | bytes 1179656 | tf_op jit(solution)/shard_map/ppermute | solution.py:55
  42.1 1.8 %shard_map.29.refs_2_ = f32[3,8,128]{2,1,0:T(8,128)S(1)} custom-call(bf16[4,24,128]{2,1,0:T(8,128)(2,1)S(1)} %shard_map.28.refs_0_, bf16[16,4,24,128]{3,2,1,0:T(8,128)(2,1)S(1)} %all_to_all.11.refs_1_), custom_call_target="tpu_custom_call" | custom-call | flops 30000000 | bytes 500000 | tf_op jit(solution)/shard_map/pallas_call | solution.py:162
  43.9 0.0 collective-permute-done.refs_1_
  43.9 2.4 %shard_map.30 = f32[3,8,128]{2,1,0:T(8,128)} custom-call(bf16[4,24,128]{2,1,0:T(8,128)(2,1)S(1)} %shard_map.28.refs_0_, bf16[16,4,24,128]{3,2,1,0:T(8,128)(2,1)S(1)} %collective-permute-done.refs_1_, f32[3,8,128]{2,1,0:T(8,128)S(1)} %shard_map.29.refs_2_), custom_call_target="tpu_custom_call" | custom-call | flops 30000000 | bytes 500000 | tf_op jit(solution)/shard_map/pallas_call | solution.py:162
Async XLA Ops:
  37.5 6.4 %collective-permute-start = (bf16[16,4,24,128]{3,2,1,0:T(8,128)(2,1)S(1)}, bf16[16,4,24,128]{3,2,1,0:T(8,128)(2,1)S(1)}, u32[]{:S(2)}, u32[]{:S(2)}) collective-permute-start(bf16[16,4,24,128]{3,2,1,0:T(8,128)(2,1)S(1)} %all_to_all.11.refs_1_), channel_id=1, source_target_pairs={{0,8},{8,0},{16,24},{24,16},{32,40},{40,32},{48,56},{56,48},{64,72... | collective-permute-start | bytes 1179656 | tf_op jit(solution)/shard_map/ppermute | solution.py:55

commit v4 on v3

--- a/solution.py
+++ b/solution.py
@@ -13,6 +13,7 @@
 ROW_TILES = 4
 LANES = 128
 ROWS = 24
+SET_ROWS = 72
 ROW_CHUNK = 16
 COL_CHUNK = 256
 SCALES = (math.sqrt(3) / 0.35, math.sqrt(3) / 0.35, math.sqrt(3) / 0.25)
@@ -37,7 +38,7 @@
     return lax.all_to_all(copies, ("grp", "tile"), 0, 0, axis_index_groups=sets)
 
 
-def within_plane(block):
+def within_plane(copies):
     planes = [
         [
             device_at(plane, 2 * m + core, c)
@@ -47,7 +48,6 @@
         for plane in range(PLANES)
         for core in range(2)
     ]
-    copies = jnp.broadcast_to(block[None], (len(planes[0]),) + block.shape)
     return lax.all_to_all(copies, ("grp", "tile"), 0, 0, axis_index_groups=planes)
 
 
@@ -82,9 +82,33 @@
     )(points, probes)
 
 
-def unpack(block):
-    wide = block.astype(jnp.float32)
-    return wide[0:8], (wide[8:11] + wide[12:15]) + wide[16:19]
+def gather_kernel(set_ref, out_ref):
+    wide = [set_ref[b].astype(jnp.float32) for b in (0, 2, 1, 3)]
+    packed = jnp.concatenate(
+        [block[0:8] for block in wide]
+        + [block[at : at + 3] for at in (8, 12, 16) for block in wide]
+        + [jnp.zeros((4, LANES), jnp.float32)],
+        0,
+    ).astype(jnp.bfloat16)
+    for copy in range(out_ref.shape[0]):
+        out_ref[copy] = packed
+
+
+def gather(blocks):
+    return pl.pallas_call(
+        gather_kernel,
+        out_shape=jax.ShapeDtypeStruct((16, SET_ROWS, LANES), jnp.bfloat16),
+        in_specs=[pl.BlockSpec(memory_space=pltpu.VMEM)],
+        out_specs=pl.BlockSpec(memory_space=pltpu.VMEM),
+        compiler_params=pltpu.CompilerParams(vmem_limit_bytes=2**20),
+    )(blocks)
+
+
+def unpack(message, kind):
+    wide = message.astype(jnp.float32)
+    coords = (wide[32:44] + wide[44:56]) + wide[56:68]
+    first = kind == 0
+    return jnp.where(first, wide[0:16], wide[16:32]), jnp.where(first, coords[0:6], coords[6:12])
 
 
 def products_kernel(first, *refs):
@@ -92,7 +116,8 @@
         own_ref, far_ref, out_ref, rows_ref, tile_ref = refs
     else:
         own_ref, far_ref, before_ref, out_ref, rows_ref, tile_ref = refs
-    own = unpack(own_ref[0])[1]
+    wide = own_ref[0].astype(jnp.float32)
+    own = (wide[8:11] + wide[12:15]) + wide[16:19]
     centre = own[:, 0:1]
     upright = jnp.transpose(jnp.concatenate([own, jnp.zeros((5, LANES), jnp.float32)], 0))
     for k in range(3):
@@ -125,17 +150,19 @@
         twin = lax.rem(group + 2, 4) + jnp.where(group < 4, 4, 0)
         place = jnp.where(inside, group, twin) // 2
         kind = jnp.where(group < 4, 1, 0)
-        for half in range(2):
-            for part in range(ROW_TILES // blocks):
-                cells = [
-                    unpack(far_ref[place * ROW_TILES + part * blocks + w, 2 * half + kind])
-                    for w in range(blocks)
-                ]
-                probe = jnp.concatenate([cell[0] for cell in cells], 1).astype(jnp.bfloat16)
+        for part in range(ROW_TILES // blocks):
+            cells = [
+                unpack(far_ref[place * ROW_TILES + part * blocks + w], kind) for w in range(blocks)
+            ]
+            for half in range(2):
+                probe = jnp.concatenate(
+                    [cell[0][half * 8 : half * 8 + 8] for cell in cells], 1
+                ).astype(jnp.bfloat16)
                 cols = [
                     [
                         jnp.broadcast_to(
-                            (cell[1][k : k + 1] - centre[k : k + 1]) * SCALES[k],
+                            (cell[1][half * 3 + k : half * 3 + k + 1] - centre[k : k + 1])
+                            * SCALES[k],
                             (ROW_CHUNK, LANES),
                         )
                         for k in range(3)
@@ -175,7 +202,7 @@
 
 def body(points, probes):
     own = pack(points, probes)
-    same = within_plane(across_planes(own))
+    same = within_plane(gather(across_planes(own)))
     swapped = other_core(same)
     return products(own, swapped, products(own, same))
 

time: 46.5 us -> 45.9 us (0.987)
  blocking collectives: 36.7 us -> 36.2 us
    all_to_all x1, blocking collectives: 11.5 us -> 10.9 us  [within_plane(): lax.all_to_all(copies, ('grp', 'tile'), 0, 0, axis_index_groups=planes)]
where the time goes in v4:
time: 45.9 us; the launch traced here: 45.7 us
  blocking collectives  36.2 us (79%)
  Pallas kernels  4.87 us (11%)
  starting transfers between devices  4.63 us (10%)
    all_to_all x1, blocking collectives, across_planes(): return lax.all_to_all(copies, ('grp', 'tile'), 0, 0, axis_index_groups=sets)  25.2 us
    all_to_all x1, blocking collectives, within_plane(): lax.all_to_all(copies, ('grp', 'tile'), 0, 0, axis_index_groups=planes)  10.9 us
    ppermute x1, starting transfers between devices, other_core(): return lax.ppermute(block, 'grp', [(i, i ^ 1) for i in range(64)])  4.63 us
    pallas_call x2, Pallas kernels, products(): pl.pallas_call(lambda *refs: products_kernel(before is None, *refs), out_...  4.13 us
  transfers between devices with their start and end apart: 1, of which 0 were waited for; matrix products, arithmetic and copies ran while one was open for 0% of the time, Pallas kernels for 4%

profile of v4, /device:TPU:1, one launch (start us, length us, event | category | flops | bytes accessed | tf_op | source)
XLA Modules:
  0.0 45.7 jit_solution(2089225172122859564)
XLA Ops:
  0.0 0.7 %shard_map.28.refs_0_ = bf16[4,24,128]{2,1,0:T(8,128)(2,1)S(1)} custom-call(f32[3,128]{1,0:T(4,128)} %points_ref.1, bf16[8,128]{1,0:T(8,128)(2,1)} %probes_ref.1), custom_call_target="tpu_custom_call" | custom-call | tf_op jit(solution)/shard_map/pallas_call | solution.py:76
  0.7 25.2 %all_to_all.10.set_ref = bf16[4,24,128]{2,1,0:T(8,128)(2,1)S(1)} all-to-all(bf16[4,24,128]{2,1,0:T(8,128)(2,1)S(1)} %shard_map.28.refs_0_), channel_id=1, replica_groups={{36,84,32,80},{37,85,33,81},{38,86,34,82},{39,87,35,83},{44,92,40,88},{..., dimensions={0} | all-to-all | bytes 49152 | tf_op jit(solution)/shard_map/all_to_all | solution.py:38
  26.0 10.9 %all_to_all.11.refs_1_ = bf16[16,72,128]{2,1,0:T(8,128)(2,1)S(1)} all-to-all(bf16[16,72,128]{2,1,0:T(8,128)(2,1)S(1)} %shard_map.29), channel_id=1, replica_groups={{2,3,0,1,18,19,16,17,34,35,32,33,50,51,48,49},{10,11,8,9,26,27,24,25,42..., dimensions={0} | all-to-all | bytes 589824 | tf_op jit(solution)/shard_map/all_to_all | solution.py:51
  36.9 4.6 %collective-permute-start = (bf16[16,72,128]{2,1,0:T(8,128)(2,1)S(1)}, bf16[16,72,128]{2,1,0:T(8,128)(2,1)S(1)}, u32[]{:S(2)}, u32[]{:S(2)}) collective-permute-start(bf16[16,72,128]{2,1,0:T(8,128)(2,1)S(1)} %all_to_all.11.refs_1_), channel_id=1, source_target_pairs={{0,8},{8,0},{16,24},{24,16},{32,40},{40,32},{48,56},{56,48},{64,72... | collective-permute-start | bytes 884744 | tf_op jit(solution)/shard_map/ppermute | solution.py:55
  41.5 1.7 %shard_map.30.refs_2_ = f32[3,8,128]{2,1,0:T(8,128)S(1)} custom-call(bf16[4,24,128]{2,1,0:T(8,128)(2,1)S(1)} %shard_map.28.refs_0_, bf16[16,72,128]{2,1,0:T(8,128)(2,1)S(1)} %all_to_all.11.refs_1_), custom_call_target="tpu_custom_call" | custom-call | flops 30000000 | bytes 500000 | tf_op jit(solution)/shard_map/pallas_call | solution.py:189
  43.3 0.0 collective-permute-done.refs_1_
  43.3 2.4 %shard_map.31 = f32[3,8,128]{2,1,0:T(8,128)} custom-call(bf16[4,24,128]{2,1,0:T(8,128)(2,1)S(1)} %shard_map.28.refs_0_, bf16[16,72,128]{2,1,0:T(8,128)(2,1)S(1)} %collective-permute-done.refs_1_, f32[3,8,128]{2,1,0:T(8,128)S(1)} %shard_map.30.refs_2_), custom_call_target="tpu_custom_call" | custom-call | flops 30000000 | bytes 500000 | tf_op jit(solution)/shard_map/pallas_call | solution.py:189
  (1 shorter events, 0.0 us)
Async XLA Ops:
  36.9 6.4 %collective-permute-start = (bf16[16,72,128]{2,1,0:T(8,128)(2,1)S(1)}, bf16[16,72,128]{2,1,0:T(8,128)(2,1)S(1)}, u32[]{:S(2)}, u32[]{:S(2)}) collective-permute-start(bf16[16,72,128]{2,1,0:T(8,128)(2,1)S(1)} %all_to_all.11.refs_1_), channel_id=1, source_target_pairs={{0,8},{8,0},{16,24},{24,16},{32,40},{40,32},{48,56},{56,48},{64,72... | collective-permute-start | bytes 884744 | tf_op jit(solution)/shard_map/ppermute | solution.py:55

commit v5 on v4

--- a/solution.py
+++ b/solution.py
@@ -109,6 +109,30 @@
     coords = (wide[32:44] + wide[44:56]) + wide[56:68]
     first = kind == 0
     return jnp.where(first, wide[0:16], wide[16:32]), jnp.where(first, coords[0:6], coords[6:12])
+
+
+def early_kernel(own_ref, far_ref, out_ref, rows_ref, tile_ref):
+    core = lax.rem(lax.axis_index("grp"), 2)
+
+    @pl.when(core == 1)
+    def _():
+        products_kernel(True, own_ref, far_ref, out_ref, rows_ref, tile_ref)
+
+    @pl.when(core == 0)
+    def _():
+        out_ref[...] = jnp.zeros(out_ref.shape, jnp.float32)
+
+
+def late_kernel(own_ref, far_ref, before_ref, out_ref, rows_ref, tile_ref):
+    core = lax.rem(lax.axis_index("grp"), 2)
+
+    @pl.when(core == 0)
+    def _():
+        products_kernel(True, own_ref, far_ref, out_ref, rows_ref, tile_ref)
+
+    @pl.when(core == 1)
+    def _():
+        out_ref[...] = before_ref[...]
 
 
 def products_kernel(first, *refs):
@@ -184,10 +208,9 @@
         out_ref[k] = total[:, k * LANES : (k + 1) * LANES]
 
 
-def products(own, far, before=None):
-    operands = (own, far) if before is None else (own, far, before)
+def products(kernel, *operands):
     return pl.pallas_call(
-        lambda *refs: products_kernel(before is None, *refs),
+        kernel,
         out_shape=jax.ShapeDtypeStruct((3, 8, LANES), jnp.float32),
         in_specs=[pl.BlockSpec(memory_space=pltpu.VMEM)] * len(operands),
         out_specs=pl.BlockSpec(memory_space=pltpu.VMEM),
@@ -203,8 +226,10 @@
 def body(points, probes):
     own = pack(points, probes)
     same = within_plane(gather(across_planes(own)))
+    same, early = lax.optimization_barrier((same, products(early_kernel, own, same)))
     swapped = other_core(same)
-    return products(own, swapped, products(own, same))
+    half = products(late_kernel, own, same, early)
+    return products(lambda *refs: products_kernel(False, *refs), own, swapped, half)
 
 
 def solution(mesh):

time: 45.9 us -> 45.3 us (0.987)
  starting transfers between devices: 4.63 us -> 2.9 us
  waiting for transfers between devices: 0.01 us -> 1.16 us
    ppermute x1, starting transfers between devices: 4.63 us -> 2.9 us  [other_core(): return lax.ppermute(block, 'grp', [(i, i ^ 1) for i in range(64)])]
    ppermute x1, waiting for transfers between devices: 0.01 us -> 1.16 us  [other_core(): return lax.ppermute(block, 'grp', [(i, i ^ 1) for i in range(64)])]
    pallas_call x2 -> x3, Pallas kernels: 4.13 us -> 4.11 us  [products(): pl.pallas_call(kernel, out_shape=jax.ShapeDtypeStruct((3, 8, LANES), jnp....]
  transfers between devices with their start and end apart: 1 -> 1, of which waited for: 0 -> 1; matrix products, arithmetic and copies ran while one was open for 0% -> 0% of each run, Pallas kernels for 4% -> 0%
where the time goes in v5:
time: 45.3 us; the launch traced here: 45.1 us
  blocking collectives  36.2 us (80%)
  Pallas kernels  4.85 us (11%)
  starting transfers between devices  2.9 us (6%)
  waiting for transfers between devices  1.16 us (3%)
    all_to_all x1, blocking collectives, across_planes(): return lax.all_to_all(copies, ('grp', 'tile'), 0, 0, axis_index_groups=sets)  25.2 us
    all_to_all x1, blocking collectives, within_plane(): lax.all_to_all(copies, ('grp', 'tile'), 0, 0, axis_index_groups=planes)  10.9 us
    pallas_call x3, Pallas kernels, products(): pl.pallas_call(kernel, out_shape=jax.ShapeDtypeStruct((3, 8, LANES), jnp....  4.11 us
    ppermute x1, starting transfers between devices, other_core(): return lax.ppermute(block, 'grp', [(i, i ^ 1) for i in range(64)])  2.9 us
    ppermute x1, waiting for transfers between devices, other_core(): return lax.ppermute(block, 'grp', [(i, i ^ 1) for i in range(64)])  1.16 us
  transfers between devices with their start and end apart: 1, of which 1 were waited for; matrix products, arithmetic and copies ran while one was open for 0% of the time, Pallas kernels for 0%

profile of v5, /device:TPU:1, one launch (start us, length us, event | category | flops | bytes accessed | tf_op | source)
XLA Modules:
  0.0 45.1 jit_solution(4889087030114862312)
XLA Ops:
  0.0 0.7 %shard_map.28.own_ref.refs_0_ = bf16[4,24,128]{2,1,0:T(8,128)(2,1)S(1)} custom-call(f32[3,128]{1,0:T(4,128)} %points_ref.1, bf16[8,128]{1,0:T(8,128)(2,1)} %probes_ref.1), custom_call_target="tpu_custom_call" | custom-call | tf_op jit(solution)/shard_map/pallas_call | solution.py:76
  0.7 25.2 %all_to_all.10.set_ref = bf16[4,24,128]{2,1,0:T(8,128)(2,1)S(1)} all-to-all(bf16[4,24,128]{2,1,0:T(8,128)(2,1)S(1)} %shard_map.28.own_ref.refs_0_), channel_id=1, replica_groups={{36,84,32,80},{37,85,33,81},{38,86,34,82},{39,87,35,83},{44,92,40,88},{..., dimensions={0} | all-to-all | bytes 49152 | tf_op jit(solution)/shard_map/all_to_all | solution.py:38
  26.0 10.9 %all_to_all.11.far_ref = bf16[16,72,128]{2,1,0:T(8,128)(2,1)S(1)} all-to-all(bf16[16,72,128]{2,1,0:T(8,128)(2,1)S(1)} %shard_map.29), channel_id=1, replica_groups={{2,3,0,1,18,19,16,17,34,35,32,33,50,51,48,49},{10,11,8,9,26,27,24,25,42..., dimensions={0} | all-to-all | bytes 589824 | tf_op jit(solution)/shard_map/all_to_all | solution.py:51
  36.9 1.7 %shard_map.30.before_ref = f32[3,8,128]{2,1,0:T(8,128)S(1)} custom-call(bf16[4,24,128]{2,1,0:T(8,128)(2,1)S(1)} %shard_map.28.own_ref.refs_0_, bf16[16,72,128]{2,1,0:T(8,128)(2,1)S(1)} %all_to_all.11.far_ref), custom_call_target="tpu_custom_call" | custom-call | flops 30000000 | bytes 500000 | tf_op jit(solution)/shard_map/pallas_call | solution.py:212
  38.6 2.9 %collective-permute-start = (bf16[16,72,128]{2,1,0:T(8,128)(2,1)S(1)}, bf16[16,72,128]{2,1,0:T(8,128)(2,1)S(1)}, u32[]{:S(2)}, u32[]{:S(2)}) collective-permute-start(bf16[16,72,128]{2,1,0:T(8,128)(2,1)S(1)} %all_to_all.11.far_ref), channel_id=1, source_target_pairs={{0,8},{8,0},{16,24},{24,16},{32,40},{40,32},{48,56},{56,48},{64,72... | collective-permute-start | bytes 884744 | tf_op jit(solution)/shard_map/ppermute | solution.py:55
  41.6 1.2 %collective-permute-done.refs_1_ = bf16[16,72,128]{2,1,0:T(8,128)(2,1)S(1)} collective-permute-done((bf16[16,72,128]{2,1,0:T(8,128)(2,1)S(1)}, bf16[16,72,128]{2,1,0:T(8,128)(2,1)S(1)}, u32[]{:S(2)}, u32[]{:S(2)}) %collective-permute-start) | collective-permute-done | bytes 294944 | tf_op jit(solution)/shard_map/ppermute | solution.py:55
  42.7 2.4 %shard_map.32 = f32[3,8,128]{2,1,0:T(8,128)} custom-call(bf16[4,24,128]{2,1,0:T(8,128)(2,1)S(1)} %shard_map.28.own_ref.refs_0_, bf16[16,72,128]{2,1,0:T(8,128)(2,1)S(1)} %collective-permute-done.refs_1_, f32[3,8,128]{2,1,0:T(8,128)S(1)} %shard_map.31.refs_2_), custom_call_target="tpu_custom_call" | custom-call | flops 30000000 | bytes 500000 | tf_op jit(solution)/shard_map/pallas_call | solution.py:212
  (2 shorter events, 0.1 us)
Async XLA Ops:
  38.6 4.1 %collective-permute-start = (bf16[16,72,128]{2,1,0:T(8,128)(2,1)S(1)}, bf16[16,72,128]{2,1,0:T(8,128)(2,1)S(1)}, u32[]{:S(2)}, u32[]{:S(2)}) collective-permute-start(bf16[16,72,128]{2,1,0:T(8,128)(2,1)S(1)} %all_to_all.11.far_ref), channel_id=1, source_target_pairs={{0,8},{8,0},{16,24},{24,16},{32,40},{40,32},{48,56},{56,48},{64,72... | collective-permute-start | bytes 884744 | tf_op jit(solution)/shard_map/ppermute | solution.py:55

commit v6 on v5

--- a/solution.py
+++ b/solution.py
@@ -15,7 +15,7 @@
 ROWS = 24
 SET_ROWS = 72
 ROW_CHUNK = 16
-COL_CHUNK = 256
+COL_CHUNK = 512
 SCALES = (math.sqrt(3) / 0.35, math.sqrt(3) / 0.35, math.sqrt(3) / 0.25)
 
 

time: 45.3 us -> 45.3 us (level)
  no operation moved by 1% of the time
where the time goes in v6:
time: 45.3 us; the launch traced here: 45.1 us
  blocking collectives  36.2 us (80%)
  Pallas kernels  4.87 us (11%)
  starting transfers between devices  2.89 us (6%)
  waiting for transfers between devices  1.16 us (3%)
    all_to_all x1, blocking collectives, across_planes(): return lax.all_to_all(copies, ('grp', 'tile'), 0, 0, axis_index_groups=sets)  25.2 us
    all_to_all x1, blocking collectives, within_plane(): lax.all_to_all(copies, ('grp', 'tile'), 0, 0, axis_index_groups=planes)  10.9 us
    pallas_call x3, Pallas kernels, products(): pl.pallas_call(kernel, out_shape=jax.ShapeDtypeStruct((3, 8, LANES), jnp....  4.13 us
    ppermute x1, starting transfers between devices, other_core(): return lax.ppermute(block, 'grp', [(i, i ^ 1) for i in range(64)])  2.89 us
    ppermute x1, waiting for transfers between devices, other_core(): return lax.ppermute(block, 'grp', [(i, i ^ 1) for i in range(64)])  1.16 us
  transfers between devices with their start and end apart: 1, of which 1 were waited for; matrix products, arithmetic and copies ran while one was open for 0% of the time, Pallas kernels for 0%

profile of v6, /device:TPU:1, one launch (start us, length us, event | category | flops | bytes accessed | tf_op | source)
XLA Modules:
  0.0 45.1 jit_solution(3581909120460951390)
XLA Ops:
  0.0 0.7 %shard_map.28.own_ref.refs_0_ = bf16[4,24,128]{2,1,0:T(8,128)(2,1)S(1)} custom-call(f32[3,128]{1,0:T(4,128)} %points_ref.1, bf16[8,128]{1,0:T(8,128)(2,1)} %probes_ref.1), custom_call_target="tpu_custom_call" | custom-call | tf_op jit(solution)/shard_map/pallas_call | solution.py:76
  0.7 25.2 %all_to_all.10.set_ref = bf16[4,24,128]{2,1,0:T(8,128)(2,1)S(1)} all-to-all(bf16[4,24,128]{2,1,0:T(8,128)(2,1)S(1)} %shard_map.28.own_ref.refs_0_), channel_id=1, replica_groups={{36,84,32,80},{37,85,33,81},{38,86,34,82},{39,87,35,83},{44,92,40,88},{..., dimensions={0} | all-to-all | bytes 49152 | tf_op jit(solution)/shard_map/all_to_all | solution.py:38
  26.0 10.9 %all_to_all.11.far_ref = bf16[16,72,128]{2,1,0:T(8,128)(2,1)S(1)} all-to-all(bf16[16,72,128]{2,1,0:T(8,128)(2,1)S(1)} %shard_map.29), channel_id=1, replica_groups={{2,3,0,1,18,19,16,17,34,35,32,33,50,51,48,49},{10,11,8,9,26,27,24,25,42..., dimensions={0} | all-to-all | bytes 589824 | tf_op jit(solution)/shard_map/all_to_all | solution.py:51
  36.9 1.7 %shard_map.30.before_ref = f32[3,8,128]{2,1,0:T(8,128)S(1)} custom-call(bf16[4,24,128]{2,1,0:T(8,128)(2,1)S(1)} %shard_map.28.own_ref.refs_0_, bf16[16,72,128]{2,1,0:T(8,128)(2,1)S(1)} %all_to_all.11.far_ref), custom_call_target="tpu_custom_call" | custom-call | flops 30000000 | bytes 500000 | tf_op jit(solution)/shard_map/pallas_call | solution.py:212
  38.7 2.9 %collective-permute-start = (bf16[16,72,128]{2,1,0:T(8,128)(2,1)S(1)}, bf16[16,72,128]{2,1,0:T(8,128)(2,1)S(1)}, u32[]{:S(2)}, u32[]{:S(2)}) collective-permute-start(bf16[16,72,128]{2,1,0:T(8,128)(2,1)S(1)} %all_to_all.11.far_ref), channel_id=1, source_target_pairs={{0,8},{8,0},{16,24},{24,16},{32,40},{40,32},{48,56},{56,48},{64,72... | collective-permute-start | bytes 884744 | tf_op jit(solution)/shard_map/ppermute | solution.py:55
  41.6 1.2 %collective-permute-done.refs_1_ = bf16[16,72,128]{2,1,0:T(8,128)(2,1)S(1)} collective-permute-done((bf16[16,72,128]{2,1,0:T(8,128)(2,1)S(1)}, bf16[16,72,128]{2,1,0:T(8,128)(2,1)S(1)}, u32[]{:S(2)}, u32[]{:S(2)}) %collective-permute-start) | collective-permute-done | bytes 294944 | tf_op jit(solution)/shard_map/ppermute | solution.py:55
  42.7 2.4 %shard_map.32 = f32[3,8,128]{2,1,0:T(8,128)} custom-call(bf16[4,24,128]{2,1,0:T(8,128)(2,1)S(1)} %shard_map.28.own_ref.refs_0_, bf16[16,72,128]{2,1,0:T(8,128)(2,1)S(1)} %collective-permute-done.refs_1_, f32[3,8,128]{2,1,0:T(8,128)S(1)} %shard_map.31.refs_2_), custom_call_target="tpu_custom_call" | custom-call | flops 30000000 | bytes 500000 | tf_op jit(solution)/shard_map/pallas_call | solution.py:212
  (2 shorter events, 0.1 us)
Async XLA Ops:
  38.7 4.1 %collective-permute-start = (bf16[16,72,128]{2,1,0:T(8,128)(2,1)S(1)}, bf16[16,72,128]{2,1,0:T(8,128)(2,1)S(1)}, u32[]{:S(2)}, u32[]{:S(2)}) collective-permute-start(bf16[16,72,128]{2,1,0:T(8,128)(2,1)S(1)} %all_to_all.11.far_ref), channel_id=1, source_target_pairs={{0,8},{8,0},{16,24},{24,16},{32,40},{40,32},{48,56},{56,48},{64,72... | collective-permute-start | bytes 884744 | tf_op jit(solution)/shard_map/ppermute | solution.py:55
